TPU v7x, 512 devices: a whole 4x4x16 slice. The times are simulated.
512 devices in a mesh: row: 16 (over x, y), col: 32 (over z, core).
Axes of the slice: x: 4, y: 4, z: 16, core: 2. Of those that a mesh axis runs over, the one named last changes fastest.
Arguments:
- centroids: float32 [3, 65536], P(None, ('col', 'row')), may hold values from -5 to 5, as said below
- weight: float32 [65536], P(('col', 'row')), may hold values from 0.5 to 2
- basis: float32 [4, 30, 65536], P(None, None, ('col', 'row')), may hold values from -6 to 6
Outputs:
- new_vector: float32 [4, 65536], P(None, ('col', 'row'))
- hessenberg: float32 [4, 31], replicated
Inputs may be any that keep to these rules, and one draw needn't show every extreme that they name: `centroids`: panels are numbered in order of increasing first coordinate.
All inputs are finite; a program needn't handle non-finite values.
Results may differ from a plain program's by a relative error of at most 0.0003.
Values sent between devices are 32-bit elements; how exact they have to be, the bound alone decides.
A program may use at most 64 MiB of HBM per device.

v0:
```python
import math

import jax
import jax.numpy as jnp
from jax import lax
from jax.sharding import PartitionSpec as P

core_factor = 16.0
epsilon = 1e-06


def tile_product(target, source, weight, vectors, panel_count):
    distance = (target[0][:, None] - source[0][None, :]) ** 2
    distance = distance + (target[1][:, None] - source[1][None, :]) ** 2
    distance = distance + (target[2][:, None] - source[2][None, :]) ** 2
    kernel_tile = weight[None, :] * lax.rsqrt(
        distance + core_factor * weight[None, :] / panel_count
    )
    kernel_tile = kernel_tile / jnp.sqrt(jnp.float32(panel_count))
    return jnp.einsum("rc,sc->sr", kernel_tile, vectors, precision=lax.Precision.HIGHEST)


def apply_rows(targets, sources, weight, vectors, panel_count):
    systems = vectors.shape[0]
    row_count = targets.shape[1]
    col_count = sources.shape[1]
    row_width = math.gcd(row_count, 512)
    col_width = math.gcd(col_count, 2048)
    target_blocks = targets.reshape(3, row_count // row_width, row_width).transpose(1, 0, 2)
    source_blocks = sources.reshape(3, col_count // col_width, col_width).transpose(1, 0, 2)
    weight_blocks = weight.reshape(col_count // col_width, col_width)
    vector_blocks = vectors.reshape(systems, col_count // col_width, col_width).transpose(1, 0, 2)

    def row_block(target):

        def advance(running_sum, pieces):
            source, piece_weights, piece_vectors = pieces
            return (
                running_sum
                + tile_product(target, source, piece_weights, piece_vectors, panel_count),
                None,
            )

        start_total = jnp.zeros((systems, row_width), jnp.float32)
        running_sum, _ = lax.scan(
            advance, start_total, (source_blocks, weight_blocks, vector_blocks)
        )
        return running_sum

    gathered = lax.map(row_block, target_blocks)
    return gathered.transpose(1, 0, 2).reshape(systems, row_count)


def per_device(centroids, weight, basis):
    segment = centroids.shape[1]
    panel_count = float(segment * lax.axis_size("row") * lax.axis_size("col"))
    newest = basis[:, basis.shape[1] - 1, :]
    weight_row = weight.reshape(1, segment)
    targets = lax.all_gather(centroids, "col", axis=1, tiled=True)
    piece_centers = lax.all_gather(centroids, "row", axis=1, tiled=True)
    piece_weights = lax.all_gather(weight_row, "row", axis=1, tiled=True)
    piece_vectors = lax.all_gather(newest, "row", axis=1, tiled=True)
    partial_value = apply_rows(
        targets, piece_centers, piece_weights.reshape(-1), piece_vectors, panel_count
    )
    applied = lax.psum_scatter(partial_value, "col", scatter_dimension=1, tiled=True)
    inv_count = 1.0 / panel_count
    highest = lax.Precision.HIGHEST
    first = lax.psum(
        jnp.einsum("skn,sn->sk", basis, applied, precision=highest) * inv_count, ("row", "col")
    )
    once = applied - jnp.einsum("sk,skn->sn", first, basis, precision=highest)
    second = lax.psum(
        jnp.einsum("skn,sn->sk", basis, once, precision=highest) * inv_count, ("row", "col")
    )
    twice = once - jnp.einsum("sk,skn->sn", second, basis, precision=highest)
    square = lax.psum(jnp.sum(twice * twice, axis=1) * inv_count, ("row", "col"))
    length = jnp.sqrt(square + epsilon)
    new_vector = twice / length[:, None]
    hessenberg = jnp.concatenate([first + second, length[:, None]], axis=1)
    return (new_vector, hessenberg)


def solution(mesh):
    placed = (P(None, ("col", "row")), P(("col", "row")), P(None, None, ("col", "row")))
    return jax.shard_map(
        per_device,
        mesh=mesh,
        in_specs=placed,
        out_specs=(P(None, ("col", "row")), P()),
        check_vma=False,
    )
```

profile of v0, /device:TPU:1, one launch (start us, length us, event | category | flops | bytes accessed | tf_op | source)
XLA Modules:
  0.0 572.1 jit_solution(9074396715291959459)
XLA Ops:
  7.2 19.2 %all_gather.14 = f32[3,2048]{1,0:T(4,128)S(1)} all-gather(f32[3,128]{1,0:T(4,128)} %param.5), channel_id=1, replica_groups=mesh['row'=16,'col'=32] {'row'}, dimensions={1}, use_global_device_ids=true | all-gather | bytes 26112 | tf_op jit(solution)/shard_map/all_gather | solution.py:60
  26.4 42.4 %all_gather.13 = f32[3,4096]{1,0:T(4,128)S(1)} all-gather(f32[3,128]{1,0:T(4,128)} %param.5), channel_id=1, replica_groups=mesh['row'=16,'col'=32] {'col'}, dimensions={1}, use_global_device_ids=true | all-gather | bytes 50688 | tf_op jit(solution)/shard_map/all_gather | solution.py:59
  68.8 0.7 slice.51
  69.5 15.3 %all-gather.2 = f32[16,1,128]{2,1,0:T(1,128)S(1)} all-gather(f32[1,1,128]{2,1,0:T(1,128)} %bitcast.95), channel_id=2, replica_groups=mesh['row'=16,'col'=32] {'row'}, dimensions={0}, use_global_device_ids=true | all-gather | bytes 8704 | tf_op jit(solution)/shard_map/all_gather | solution.py:61
  84.8 16.4 %all-gather.1 = f32[4,1,2048]{2,0,1:T(4,128)S(1)} all-gather(f32[4,1,128]{2,0,1:T(4,128)S(1)} %slice.51), channel_id=3, replica_groups=mesh['row'=16,'col'=32] {'row'}, dimensions={2}, use_global_device_ids=true | all-gather | bytes 34816 | tf_op jit(solution)/shard_map/all_gather | solution.py:62
  101.2 42.7 %while.16 = (s32[]{:T(128)}, f32[8,4,512]{2,1,0:T(4,128)S(1)}, f32[1,2048]{1,0:T(1,128)S(1)}, f32[8,3,512]{2,1,0:T(4,128)S(1)}, f32[1,3,2048]{2,1,0:T(4,128)S(1)...) while((s32[]{:T(128)}, f32[8,4,512]{2,1,0:T(4,128)S(1)}, f32[1,2048]{1,0:T(1,128)S(1)}, ...), condition=%wide.region_1.2_spmd, body=%wide.region_0.1_spmd.sunk | while | flops 61868036 | bytes 166037 | solution.py:50
  101.3 5.3 fusion.51
  106.6 5.3 fusion.51
  111.9 5.3 fusion.51
  117.3 5.3 fusion.51
  122.6 5.3 fusion.51
  127.9 5.3 fusion.51
  133.3 5.3 fusion.51
  138.6 5.3 fusion.51
  143.9 2.0 copy.18
  145.9 109.9 %reduce-scatter.4.cloned.1.call-done = f32[128,4]{1,0:T(8,128)} async-done(((f32[4096,4]{1,0:T(8,128)}), f32[128,4]{1,0:T(8,128)}) %reduce-scatter.4.cloned.1.call-update) | async-done | bytes 2064
  255.8 0.9 copy.19
  256.7 0.2 fusion.36
  256.9 106.5 %psum.21 = f32[4,30]{1,0:T(4,128)S(1)} all-reduce(f32[4,30]{1,0:T(4,128)S(1)} %broadcast_multiply_fusion.2), channel_id=1, replica_groups=mesh['row'=16,'col'=32] {'row','col'}, use_global_device_ids=true, to_apply=%region_3.4 | all-reduce | flops 120 | bytes 960 | tf_op jit(solution)/shard_map/psum | solution.py:69
  363.6 0.2 fusion.32
  363.9 98.4 %psum.22 = f32[4,30]{1,0:T(4,128)S(1)} all-reduce(f32[4,30]{1,0:T(4,128)S(1)} %broadcast_multiply_fusion.1), channel_id=1, replica_groups=mesh['row'=16,'col'=32] {'row','col'}, use_global_device_ids=true, to_apply=%region_4.5 | all-reduce | flops 120 | bytes 960 | tf_op jit(solution)/shard_map/psum | solution.py:73
  462.6 101.3 %psum.23 = f32[4]{0:T(128)S(1)} all-reduce(f32[4]{0:T(128)S(1)} %broadcast_multiply_fusion.3), channel_id=1, replica_groups=mesh['row'=16,'col'=32] {'row','col'}, use_global_device_ids=true, to_apply=%region_6.7 | all-reduce | flops 4 | bytes 32 | tf_op jit(solution)/shard_map/psum | solution.py:77
  563.9 0.7 broadcast_divide_fusion
  564.6 0.7 pad_maximum_fusion
  (39 shorter events, 1.0 us)
Async XLA Ops:
  7.2 248.6 %reduce-scatter.4.cloned.1.call-start = ((), (), s32[]{:S(2)}) async-start(), calls=%async_computation.1 | async-start | bytes 2162688
  143.9 112.8 %copy-start = (f32[4,30,128]{2,0,1:T(4,128)S(1)}, f32[4,30,128]{2,0,1:T(4,128)}, u32[]{:S(2)}) copy-start(f32[4,30,128]{2,0,1:T(4,128)} %param.7) | copy-start | bytes 184324
Sparse Core Ops, SparseCore 0:
  146.1 109.7 reduce-scatter.3
where the time goes:
time: 573 us; the launch traced here: 572 us
  blocking collectives  400 us (70%)
  waiting for transfers between devices  110 us (19%)
  matrix products  42.9 us (7%)
  between operations  14.1 us (2%)
    unnamed x2, waiting for transfers between devices  110 us
    psum x1, blocking collectives, per_device(): lax.psum(jnp.einsum('skn,sn->sk', basis, applied, precision=highest) * in...  107 us
    psum x1, blocking collectives, per_device(): lax.psum(jnp.sum(twice * twice, axis=1) * inv_count, ('row', 'col'))  101 us
    psum x1, blocking collectives, per_device(): lax.psum(jnp.einsum('skn,sn->sk', basis, once, precision=highest) * inv_c...  98.4 us
    all_gather x1, blocking collectives, per_device(): targets = lax.all_gather(centroids, 'col', axis=1, tiled=True)  42.4 us
    dot_general x8, matrix products, tile_product(): jnp.einsum('rc,sc->sr', kernel_tile, vectors, precision=lax.Precision.HIG...  42.1 us
    all_gather x1, blocking collectives, per_device(): piece_centers = lax.all_gather(centroids, 'row', axis=1, tiled=True)  19.2 us
    all_gather x1, blocking collectives, per_device(): piece_vectors = lax.all_gather(newest, 'row', axis=1, tiled=True)  16.4 us
  transfers between devices with their start and end apart: 1, of which 1 were waited for; matrix products, arithmetic and copies ran while one was open for 0% of the time, Pallas kernels for 0%

commit v1 on v0

v1 whole, which is shorter than its diff:
```python
import functools

import jax
import jax.numpy as jnp
import numpy as np
from jax import lax
from jax.experimental import pallas as pl
from jax.experimental.pallas import tpu as pltpu
from jax.sharding import PartitionSpec as P

MESH = pl.DeviceIdType.MESH
f32, bf16 = jnp.float32, jnp.bfloat16
HIGHEST = lax.Precision.HIGHEST

SYSTEMS = 4
KRYLOV = 30
SEG = 128
ROWS = 16
COLS = 32
PANELS = SEG * ROWS * COLS
SOURCES = ROWS * SEG
CHUNK = 256
FEATURES = 128
CORE = 16.0 / PANELS
EPSILON = 1e-06


def selections():
    source = np.zeros((FEATURES, 48), np.float32)
    target = np.zeros((FEATURES, 48), np.float32)
    coarse, fine, one = (0, 8), (16, 24), 38

    def products(at, lefts, rights):
        for left in lefts:
            for right in rights:
                for axis in range(3):
                    source[at, left + axis] = 1
                    target[at, right + axis] = -2
                    at += 1
        return at

    def norms(at, pieces):
        for piece in pieces:
            source[at, piece] = target[at, one] = 1
            source[at + 1, one] = target[at + 1, piece] = 1
            at += 2
        return at

    norms(products(0, coarse, coarse), (32, 33, 34))
    at = products(32, coarse, fine)
    at = products(at, fine, coarse + fine)
    norms(at, (35, 36, 37))
    return source, target


def rounded(a):
    return a.astype(bf16).astype(f32)


def pieces_of(points, extra):
    at = lax.broadcasted_iota(jnp.int32, (8, SEG), 0)
    points = jnp.where(at < 3, points, 0.0)
    coarse = jnp.floor(points * 128.0 + 0.5) * (1.0 / 128.0)
    fine = points - coarse
    coarse_high = rounded(coarse)
    fine_high = rounded(fine)
    fine_low = rounded(fine - fine_high)
    norm = jnp.sum(coarse * coarse, axis=0, keepdims=True)
    rest = jnp.sum(2.0 * coarse * fine + fine * fine, axis=0, keepdims=True) + extra
    tail = jnp.where(at == 6, 1.0, 0.0)
    row = 0
    for whole in (norm, rest):
        for _ in range(3):
            piece = rounded(whole)
            tail = jnp.where(at == row, piece, tail)
            whole = whole - piece
            row += 1
    rows = [coarse_high, coarse - coarse_high, fine_high, fine_low, tail, jnp.zeros((8, SEG), f32)]
    return jnp.concatenate(rows, axis=0).astype(bf16)


def contract(a, b, dims, **kw):
    return lax.dot_general(a, b, ((dims[:1], dims[1:]), ((), ())), preferred_element_type=f32, **kw)


def step_kernel(
    centroids, weight, basis, source_sel, target_sel, new_vector, hessenberg,
    src, tgt, feat, vecs, part, landed, bmat, col_buf, row_buf, send_sem, recv_sem,
):
    r, c = lax.axis_index("row"), lax.axis_index("col")
    barrier = pltpu.get_barrier_semaphore()

    @pl.loop(1, ROWS)
    def _(i):
        pl.semaphore_signal(
            barrier, inc=1, device_id=(lax.rem(r + i, ROWS), c), device_id_type=MESH
        )

    @pl.loop(1, COLS)
    def _(i):
        pl.semaphore_signal(
            barrier, inc=1, device_id=(r, lax.rem(c + i, COLS)), device_id_type=MESH
        )

    def to_rows(buf, slot, sem):
        @pl.loop(1, ROWS)
        def _(i):
            pltpu.make_async_remote_copy(
                src_ref=buf.at[slot], dst_ref=buf.at[slot],
                send_sem=send_sem.at[sem], recv_sem=recv_sem.at[sem],
                device_id=(lax.rem(r + i, ROWS), c), device_id_type=MESH,
            ).start()

    def to_cols(buf, slot, sem):
        @pl.loop(1, COLS)
        def _(i):
            pltpu.make_async_remote_copy(
                src_ref=buf.at[slot], dst_ref=buf.at[slot],
                send_sem=send_sem.at[sem], recv_sem=recv_sem.at[sem],
                device_id=(r, lax.rem(c + i, COLS)), device_id_type=MESH,
            ).start()

    def all_but_one(buf, sem):
        view = buf.at[pl.ds(0, buf.shape[0] - 1)]
        pltpu.make_async_copy(view, view, sem).wait()

    src[r, 0:3, :] = centroids[...]
    src[r, 3:4, :] = weight[...]
    for s in range(SYSTEMS):
        src[r, 4 + s : 5 + s, :] = basis[s, KRYLOV - 1 : KRYLOV, :]
    tgt[c, 0:3, :] = centroids[...]
    tgt[c, 3:4, :] = weight[...]
    bmat[...] = jnp.zeros_like(bmat)
    for s in range(SYSTEMS):
        bmat[32 * s : 32 * s + KRYLOV, :] = basis[s]

    pl.semaphore_wait(barrier, ROWS + COLS - 2)
    to_rows(src, r, 0)
    to_cols(tgt, c, 1)

    all_but_one(src, recv_sem.at[0])
    for b in range(ROWS):
        block = src[b]
        pieces = pieces_of(block, block[3:4] * CORE)
        rows = slice(b * SEG, (b + 1) * SEG)
        feat[rows, :] = contract(pieces, source_sel[...], (0, 1)).astype(bf16)
        scaled = block[4:8] * (block[3:4] * (1.0 / PANELS**0.5))
        high = rounded(scaled)
        vecs[:, rows] = jnp.concatenate(
            [high, scaled - high, jnp.zeros((8, SEG), f32)], axis=0
        ).astype(bf16)

    all_but_one(tgt, recv_sem.at[1])
    chips = COLS // 2
    chip = c // 2

    @pl.loop(0, chips)
    def _(i):
        away = chips // 2 - (i + 1) // 2
        other = lax.rem(chip + chips + away * (2 * lax.rem(i, 2) - 1), chips)
        pieces = []
        for core in range(2):
            block = jnp.concatenate([tgt[2 * other + core], jnp.zeros((4, SEG), f32)], axis=0)
            pieces.append(pieces_of(block, 0.0))
        meets = contract(target_sel[...], jnp.concatenate(pieces, axis=1), (1, 0)).astype(bf16)
        total = jnp.zeros((16, CHUNK), f32)
        for b in range(SOURCES // CHUNK):
            rows = slice(b * CHUNK, (b + 1) * CHUNK)
            entry = lax.rsqrt(contract(feat[rows, :], meets, (1, 0)))
            high = entry.astype(bf16)
            low = (entry - high.astype(f32)).astype(bf16)
            total = total + contract(vecs[:, rows], high, (1, 0))
            total = total + contract(vecs[:, rows], low, (1, 0))
        total = total[0:4] + total[4:8]
        for core in range(2):
            to = 2 * other + core
            mine = total[:, core * SEG : (core + 1) * SEG]

            @pl.when(to == c)
            def _():
                landed[c] = mine

            @pl.when(to != c)
            def _():
                part[to] = mine
                pltpu.make_async_remote_copy(
                    src_ref=part.at[to], dst_ref=landed.at[c],
                    send_sem=send_sem.at[2], recv_sem=recv_sem.at[2],
                    device_id=(r, to), device_id_type=MESH,
                ).start()

    all_but_one(landed, recv_sem.at[2])
    applied = jnp.sum(landed[...], axis=0)
    applied = jnp.concatenate([applied, jnp.zeros((4, SEG), f32)], axis=0)

    system = lax.broadcasted_iota(jnp.int32, (8, SEG), 0)
    lane = lax.broadcasted_iota(jnp.int32, (8, SEG), 1)
    own = lane // 32 == system

    def total_over_devices(local, at):
        col = col_buf.at[at]
        col[c] = local
        to_cols(col, c, 3 + 2 * at)
        all_but_one(col, recv_sem.at[3 + 2 * at])
        row = row_buf.at[at]
        row[r] = jnp.sum(col[...], axis=0)
        to_rows(row, r, 4 + 2 * at)
        all_but_one(row, recv_sem.at[4 + 2 * at])
        return jnp.sum(row[...], axis=0)

    def inner(vector):
        every = contract(vector, bmat[...], (1, 1), precision=HIGHEST)
        return jnp.sum(jnp.where(own, every, 0.0), axis=0, keepdims=True) * (1.0 / PANELS)

    def spread(coefficients):
        return jnp.where(own, jnp.broadcast_to(coefficients, (8, SEG)), 0.0)

    def along(coefficients):
        return contract(spread(coefficients), bmat[...], (1, 0), precision=HIGHEST)

    first = total_over_devices(inner(applied), 0)
    once = applied - along(first)
    second = total_over_devices(inner(once), 1)
    twice = once - along(second)
    square = jnp.sum(twice * twice, axis=1, keepdims=True) * (1.0 / PANELS)
    square = jnp.sum(jnp.where(own, jnp.broadcast_to(square, (8, SEG)), 0.0), axis=0, keepdims=True)
    square = total_over_devices(square, 2)
    length = jnp.sqrt(square + EPSILON)
    each = jnp.sum(jnp.where(lane % 32 == 0, spread(length), 0.0), axis=1, keepdims=True)
    new_vector[...] = (twice / jnp.where(system[:, 0:1] < SYSTEMS, each, 1.0))[0:SYSTEMS]
    column = jnp.where(lane[0:1] % 32 == KRYLOV, length, first + second)
    for s in range(SYSTEMS):
        hessenberg[s : s + 1, :] = column[:, 32 * s : 32 * s + KRYLOV + 1]

    all_but_one(src, send_sem.at[0])
    all_but_one(tgt, send_sem.at[1])
    all_but_one(landed, send_sem.at[2])
    for at in range(3):
        all_but_one(col_buf.at[at], send_sem.at[3 + 2 * at])
        all_but_one(row_buf.at[at], send_sem.at[4 + 2 * at])


def per_device(centroids, weight, basis):
    source, target = selections()
    vmem = pl.BlockSpec(memory_space=pltpu.VMEM)
    return pl.pallas_call(
        step_kernel,
        out_shape=(
            jax.ShapeDtypeStruct((SYSTEMS, SEG), f32),
            jax.ShapeDtypeStruct((SYSTEMS, KRYLOV + 1), f32),
        ),
        in_specs=[vmem] * 5,
        out_specs=(vmem, vmem),
        scratch_shapes=[
            pltpu.VMEM((ROWS, 8, SEG), f32),
            pltpu.VMEM((COLS, 4, SEG), f32),
            pltpu.VMEM((SOURCES, FEATURES), bf16),
            pltpu.VMEM((16, SOURCES), bf16),
            pltpu.VMEM((COLS, 4, SEG), f32),
            pltpu.VMEM((COLS, 4, SEG), f32),
            pltpu.VMEM((SEG, SEG), f32),
            pltpu.VMEM((3, COLS, 1, SEG), f32),
            pltpu.VMEM((3, ROWS, 1, SEG), f32),
            pltpu.SemaphoreType.DMA((9,)),
            pltpu.SemaphoreType.DMA((9,)),
        ],
        compiler_params=pltpu.CompilerParams(
            collective_id=0, has_side_effects=True, vmem_limit_bytes=40 * 2**20
        ),
        name="arnoldi_step",
    )(centroids, weight.reshape(1, SEG), basis, jnp.asarray(source, bf16), jnp.asarray(target, bf16))


def solution(mesh):
    placed = (P(None, ("col", "row")), P(("col", "row")), P(None, None, ("col", "row")))
    return jax.shard_map(
        per_device,
        mesh=mesh,
        in_specs=placed,
        out_specs=(P(None, ("col", "row")), P()),
        check_vma=False,
    )
```

time: 573 us -> 83.1 us (0.15)
  blocking collectives: 400 us -> 0 us
  waiting for transfers between devices: 110 us -> 0 us
  Pallas kernels: 0 us -> 80.2 us
  matrix products: 42.9 us -> 0 us
  between operations: 14.1 us -> 0.69 us
    psum x3 -> x0, blocking collectives: 306 us -> none  [the longest x1 107 us: per_device(): lax.psum(jnp.einsum('skn,sn->sk', basis, applied, precision=highest) * in...]
    unnamed x2 -> x0, waiting for transfers between devices: 110 us -> none
    all_gather x4 -> x0, blocking collectives: 93.3 us -> none  [the longest x1 42.4 us: per_device(): targets = lax.all_gather(centroids, 'col', axis=1, tiled=True)]
    pallas_call x0 -> x1, Pallas kernels: none -> 80.2 us  [per_device(): pl.pallas_call(step_kernel, out_shape=(jax.ShapeDtypeStruct((SYSTEMS, SEG...]
    dot_general x12 -> x0, matrix products: 42.9 us -> none  [the longest x8 42.1 us: tile_product(): jnp.einsum('rc,sc->sr', kernel_tile, vectors, precision=lax.Precision.HIG...]
  transfers between devices with their start and end apart: 1 -> 0, of which waited for: 1 -> 0; matrix products, arithmetic and copies ran while one was open for 0% -> 0% of each run, Pallas kernels for 0% -> 0%
where the time goes in v1:
time: 83.1 us; the launch traced here: 82.9 us
  Pallas kernels  80.2 us (97%)
  local copies, waits for them, and re-layouts  2.04 us (2%)
    pallas_call x1, Pallas kernels, per_device(): pl.pallas_call(step_kernel, out_shape=(jax.ShapeDtypeStruct((SYSTEMS, SEG...  80.2 us
    unnamed x11, local copies, waits for them, and re-layouts  2.04 us

profile of v1, /device:TPU:1, one launch (start us, length us, event | category | flops | bytes accessed | tf_op | source)
XLA Modules:
  0.0 82.9 jit_solution(14455591610076414076)
XLA Ops:
  0.6 0.0 copy-start
  0.6 0.0 copy-start.1
  0.7 0.0 copy-start.2
  0.7 0.0 copy-start.3
  0.7 0.9 %copy.7.basis = f32[4,30,128]{2,1,0:T(8,128)S(1)} copy(f32[4,30,128]{2,0,1:T(4,128)} %param.7) | data formatting | bytes 122880 | tf_op args[2]
  1.5 0.0 copy-done
  1.5 0.0 copy-done.1
  1.5 0.0 copy-done.2
  1.5 0.0 copy-done.3
  1.6 80.2 %arnoldi_step.1 = (f32[4,128]{1,0:T(4,128)S(1)}, f32[4,31]{1,0:T(4,128)S(1)}) custom-call(f32[3,128]{1,0:T(4,128)S(1)} %copy-done.2, f32[1,128]{1,0:T(1,128)S(1)} %bitcast.1, f32[4,30,128]{2,1,0:T(8,128)S(1)} %copy.7.basis, bf16[128,48]{1,0:T(8,128)(2,1)S(1)} %copy-done.1, bf16[128,48]{1,0:T(8,128)(2,1)S(1)} %copy-done), custom_call_target="tpu_custom_call" | custom-call | tf_op jit(solution)/shard_map/arnoldi_step/pallas_call | solution.py:246
  81.8 0.6 copy.10
  82.3 0.6 copy.11
Async XLA Ops:
  0.6 0.9 %copy-start = (bf16[128,48]{1,0:T(8,128)(2,1)S(1)}, bf16[128,48]{1,0:T(8,128)(2,1)}, u32[]{:S(2)}) copy-start(bf16[128,48]{1,0:T(8,128)(2,1)} %constant.5.clone.target_sel) | copy-start | bytes 36868
  0.6 0.9 %copy-start.1 = (bf16[128,48]{1,0:T(8,128)(2,1)S(1)}, bf16[128,48]{1,0:T(8,128)(2,1)}, u32[]{:S(2)}) copy-start(bf16[128,48]{1,0:T(8,128)(2,1)} %constant.4.clone.source_sel) | copy-start | bytes 36868
  0.7 0.9 %copy-start.2 = (f32[3,128]{1,0:T(4,128)S(1)}, f32[3,128]{1,0:T(4,128)}, u32[]{:S(2)}) copy-start(f32[3,128]{1,0:T(4,128)} %centroids.1) | copy-start | bytes 4612
  0.7 0.9 %copy-start.3 = (f32[128]{0:T(128)S(1)}, f32[128]{0:T(128)}, u32[]{:S(2)}) copy-start(f32[128]{0:T(128)} %param.6) | copy-start | bytes 1540

commit v2 on v1

v2 whole, which is shorter than its diff:
```python
import functools

import jax
import jax.numpy as jnp
import numpy as np
from jax import lax
from jax.experimental import pallas as pl
from jax.experimental.pallas import tpu as pltpu
from jax.sharding import PartitionSpec as P

MESH = pl.DeviceIdType.MESH
f32, bf16 = jnp.float32, jnp.bfloat16
HIGHEST = lax.Precision.HIGHEST

SYSTEMS = 4
KRYLOV = 30
SEG = 128
ROWS = 16
COLS = 32
PANELS = SEG * ROWS * COLS
SOURCES = ROWS * SEG
CHUNK = 256
FEATURES = 128
CORE = 16.0 / PANELS
DEPTH = 16
PLANE = 32
NEAR = 8
DEPTH = 16
PLANE = 32
NEAR = 8
EPSILON = 1e-06


def selections():
    source = np.zeros((FEATURES, 48), np.float32)
    target = np.zeros((FEATURES, 48), np.float32)
    coarse, fine, one = (0, 8), (16, 24), 38

    def products(at, lefts, rights):
        for left in lefts:
            for right in rights:
                for axis in range(3):
                    source[at, left + axis] = 1
                    target[at, right + axis] = -2
                    at += 1
        return at

    def norms(at, pieces):
        for piece in pieces:
            source[at, piece] = target[at, one] = 1
            source[at + 1, one] = target[at + 1, piece] = 1
            at += 2
        return at

    norms(products(0, coarse, coarse), (32, 33, 34))
    at = products(32, coarse, fine)
    at = products(at, fine, coarse + fine)
    norms(at, (35, 36, 37))
    return source, target


def rounded(a):
    return a.astype(bf16).astype(f32)


def pieces_of(points, extra):
    at = lax.broadcasted_iota(jnp.int32, (8, SEG), 0)
    points = jnp.where(at < 3, points, 0.0)
    coarse = jnp.floor(points * 128.0 + 0.5) * (1.0 / 128.0)
    fine = points - coarse
    coarse_high = rounded(coarse)
    fine_high = rounded(fine)
    fine_low = rounded(fine - fine_high)
    norm = jnp.sum(coarse * coarse, axis=0, keepdims=True)
    rest = jnp.sum(2.0 * coarse * fine + fine * fine, axis=0, keepdims=True) + extra
    tail = jnp.where(at == 6, 1.0, 0.0)
    row = 0
    for whole in (norm, rest):
        for _ in range(3):
            piece = rounded(whole)
            tail = jnp.where(at == row, piece, tail)
            whole = whole - piece
            row += 1
    rows = [coarse_high, coarse - coarse_high, fine_high, fine_low, tail, jnp.zeros((8, SEG), f32)]
    return jnp.concatenate(rows, axis=0).astype(bf16)


def contract(a, b, dims, **kw):
    return lax.dot_general(a, b, ((dims[:1], dims[1:]), ((), ())), preferred_element_type=f32, **kw)


def two_sum(a,b):
    s=a+b
    t=s-a
    return s,(a-(s-t))+(b-t)
def pair_sum(p,q):
    s,e=two_sum(p[0],q[0])
    e=e+(p[1]+q[1])
    h=s+e
    return h,e-(h-s)
def pair_product(a,b):
    p=a*b
    ah,bh=rounded(a),rounded(b)
    al,bl=a-ah,b-bh
    return p,((ah*bh-p)+ah*bl+al*bh)+al*bl
def fold(parts):
    while len(parts)>1:
        parts=[pair_sum(*parts[i:i+2]) if i+1<len(parts) else parts[i] for i in range(0,len(parts),2)]
    return parts[0]
def down(p):
    m=p[0].shape[0]//8
    p=fold([(p[0][8*i:8*i+8],p[1][8*i:8*i+8]) for i in range(m)])
    for by in (4,2,1):
        p=pair_sum(p,(pltpu.roll(p[0],by,0),pltpu.roll(p[1],by,0)))
    return p[0][0:1],p[1][0:1]
def across(by_row):
    lane=lax.broadcasted_iota(jnp.int32,(32,SEG),1)//32
    out=by_row[0:32]
    for s in range(1,SYSTEMS):
        out=jnp.where(lane==s,by_row[32*s:32*s+32],out)
    return out
def gram(b):
    slices=[]
    rest=b
    for bits in (4,12,20,28):
        q=jnp.floor(rest*2.0**bits+0.5)*2.0**-bits
        rest=rest-q
        slices.append(q.astype(bf16))
    total=None
    for level in range(5):
        pairs=[(i,level-i) for i in range(4) if 0<=level-i<4]
        left=jnp.concatenate([slices[i] for i,_ in pairs],axis=1)
        right=jnp.concatenate([slices[j] for _,j in pairs],axis=1)
        part=across(contract(left,right,(1,1)))
        exact=(part,jnp.zeros_like(part))
        total=exact if total is None else pair_sum(total,exact)
    return total[0]*(1.0/PANELS),total[1]*(1.0/PANELS)
def payload(a,bt):
    lane=lax.broadcasted_iota(jnp.int32,(SEG,SEG),1)%32
    at=jnp.concatenate([jnp.broadcast_to(a[s:s+1],(32,SEG)) for s in range(SYSTEMS)],axis=0).T
    h,l=down(pair_product(at,jnp.where(lane==KRYLOV,at,bt)))
    return h*(1.0 / PANELS),l*(1.0 / PANELS)
def finish(a,p,g,bmat):
    k=lax.broadcasted_iota(jnp.int32,(1,SEG),1)%32
    system=lax.broadcasted_iota(jnp.int32,(8,SEG),0)
    lane=lax.broadcasted_iota(jnp.int32,(8,SEG),1)
    own=lane//32==system
    def times(c):
        column=across(jnp.broadcast_to(c,(SEG,SEG)).T)
        h,l=pair_product(g[0],column)
        return down((h,l+g[1]*column))
    basis_lane=k<KRYLOV
    fh,fl=jnp.where(basis_lane,p[0],0.0),jnp.where(basis_lane,p[1],0.0)
    gf=times(fh)
    second=(fh-gf[0])+(fl-gf[1])
    c=fh+second
    a8=jnp.concatenate([a,jnp.zeros((4,SEG),f32)],axis=0)
    twice=a8-contract(jnp.where(own,jnp.broadcast_to(c,(8,SEG)),0.0),bmat,(1,0),precision=HIGHEST)
    gc=times(c)
    u=pair_sum(gc,(-2.0*fh,-2.0*fl))
    h,l=pair_product(c,u[0])
    l=l+c*u[1]
    square=(jnp.where(k==KRYLOV,p[0],h),jnp.where(k==KRYLOV,p[1],l))
    for by in (1,2,4,8,16):
        square=pair_sum(square,(pltpu.roll(square[0],by,1),pltpu.roll(square[1],by,1)))
    length=jnp.sqrt(jnp.maximum(square[0]+square[1],0.0)+EPSILON)
    each=jnp.sum(jnp.where(own&(lane%32==31),jnp.broadcast_to(length,(8,SEG)),0.0),axis=1,keepdims=True)
    new=(twice/jnp.where(system[:,0:1]<SYSTEMS,each,1.0))[0:SYSTEMS]
    return new,jnp.where(k==KRYLOV,pltpu.roll(length,SEG-1,1),c)


def load_basis(basis,bmat):
    bmat[...]=jnp.zeros_like(bmat)
    for s in range(SYSTEMS):
        bmat[32*s:32*s+KRYLOV,:]=basis[s]
def two_sum(a,b):
    s=a+b
    t=s-a
    return s,(a-(s-t))+(b-t)
def pair_sum(p,q):
    s,e=two_sum(p[0],q[0])
    e=e+(p[1]+q[1])
    h=s+e
    return h,e-(h-s)
def pair_product(a,b):
    p=a*b
    ah,bh=rounded(a),rounded(b)
    al,bl=a-ah,b-bh
    return p,((ah*bh-p)+ah*bl+al*bh)+al*bl
def fold(parts):
    while len(parts)>1:
        parts=[pair_sum(*parts[i:i+2]) if i+1<len(parts) else parts[i] for i in range(0,len(parts),2)]
    return parts[0]
def down(p):
    m=p[0].shape[0]//8
    p=fold([(p[0][8*i:8*i+8],p[1][8*i:8*i+8]) for i in range(m)])
    for by in (4,2,1):
        p=pair_sum(p,(pltpu.roll(p[0],by,0),pltpu.roll(p[1],by,0)))
    return p[0][0:1],p[1][0:1]
def across(by_row):
    lane=lax.broadcasted_iota(jnp.int32,(32,SEG),1)//32
    out=by_row[0:32]
    for s in range(1,SYSTEMS):
        out=jnp.where(lane==s,by_row[32*s:32*s+32],out)
    return out
def gram(b):
    slices=[]
    rest=b
    for bits in (4,12,20,28):
        q=jnp.floor(rest*2.0**bits+0.5)*2.0**-bits
        rest=rest-q
        slices.append(q.astype(bf16))
    total=None
    for level in range(5):
        pairs=[(i,level-i) for i in range(4) if 0<=level-i<4]
        left=jnp.concatenate([slices[i] for i,_ in pairs],axis=1)
        right=jnp.concatenate([slices[j] for _,j in pairs],axis=1)
        part=across(contract(left,right,(1,1)))
        exact=(part,jnp.zeros_like(part))
        total=exact if total is None else pair_sum(total,exact)
    return total[0]*(1.0/PANELS),total[1]*(1.0/PANELS)
def payload(a,bt):
    lane=lax.broadcasted_iota(jnp.int32,(SEG,SEG),1)%32
    at=jnp.concatenate([jnp.broadcast_to(a[s:s+1],(32,SEG)) for s in range(SYSTEMS)],axis=0).T
    h,l=down(pair_product(at,jnp.where(lane==KRYLOV,at,bt)))
    return h*(1.0 / PANELS),l*(1.0 / PANELS)
def finish(a,p,g,bmat):
    k=lax.broadcasted_iota(jnp.int32,(1,SEG),1)%32
    system=lax.broadcasted_iota(jnp.int32,(8,SEG),0)
    lane=lax.broadcasted_iota(jnp.int32,(8,SEG),1)
    own=lane//32==system
    def times(c):
        column=across(jnp.broadcast_to(c,(SEG,SEG)).T)
        h,l=pair_product(g[0],column)
        return down((h,l+g[1]*column))
    basis_lane=k<KRYLOV
    fh,fl=jnp.where(basis_lane,p[0],0.0),jnp.where(basis_lane,p[1],0.0)
    gf=times(fh)
    second=(fh-gf[0])+(fl-gf[1])
    c=fh+second
    a8=jnp.concatenate([a,jnp.zeros((4,SEG),f32)],axis=0)
    twice=a8-contract(jnp.where(own,jnp.broadcast_to(c,(8,SEG)),0.0),bmat,(1,0),precision=HIGHEST)
    gc=times(c)
    u=pair_sum(gc,(-2.0*fh,-2.0*fl))
    h,l=pair_product(c,u[0])
    l=l+c*u[1]
    square=(jnp.where(k==KRYLOV,p[0],h),jnp.where(k==KRYLOV,p[1],l))
    for by in (1,2,4,8,16):
        square=pair_sum(square,(pltpu.roll(square[0],by,1),pltpu.roll(square[1],by,1)))
    length=jnp.sqrt(jnp.maximum(square[0]+square[1],0.0)+EPSILON)
    each=jnp.sum(jnp.where(own&(lane%32==31),jnp.broadcast_to(length,(8,SEG)),0.0),axis=1,keepdims=True)
    new=(twice/jnp.where(system[:,0:1]<SYSTEMS,each,1.0))[0:SYSTEMS]
    return new,jnp.where(k==KRYLOV,pltpu.roll(length,SEG-1,1),c)


def step_kernel(
    centroids, weight, basis, source_sel, target_sel, new_vector, hessenberg,
    src, tgt, feat, meet, vecs, sums, part, landed, bmat, bmat_t, gram_out, gram_in, gram_z, gram_all,
    dots_z, dots_q, send_sem, recv_sem,
):
    r, c = lax.axis_index("row"), lax.axis_index("col")
    z, q = c // 2, 2 * r + lax.rem(c, 2)

    def on_line(i):
        return r, lax.rem(c + 2 * i, 2 * DEPTH)

    def on_plane(to):
        return to // 2, 2 * z + lax.rem(to, 2)

    barrier = pltpu.get_barrier_semaphore()

    @pl.loop(1, DEPTH)
    def _(i):
        pl.semaphore_signal(barrier, inc=1, device_id=on_line(i), device_id_type=MESH)

    @pl.loop(1, PLANE)
    def _(i):
        pl.semaphore_signal(
            barrier, inc=1, device_id=on_plane(lax.rem(q + i, PLANE)), device_id_type=MESH
        )

    def send(piece, place, sem, device):
        pltpu.make_async_remote_copy(
            src_ref=piece, dst_ref=place, send_sem=send_sem.at[sem], recv_sem=recv_sem.at[sem],
            device_id=device, device_id_type=MESH,
        ).start()

    def to_line(buf, sem):
        @pl.loop(1, DEPTH)
        def _(i):
            send(buf.at[z], buf.at[z], sem, on_line(i))

    def to_plane(buf, sem):
        @pl.loop(1, PLANE)
        def _(i):
            send(buf.at[q], buf.at[q], sem, on_plane(lax.rem(q + i, PLANE)))

    def settle(buf, count, sem):
        view = buf.at[pl.ds(0, count)]
        pltpu.make_async_copy(view, view, sem).wait()

    own_slot = 3
    src[own_slot, 0:3, :] = centroids[...]
    src[own_slot, 3:4, :] = weight[...]
    for s in range(SYSTEMS):
        src[own_slot, 4 + s : 5 + s, :] = basis[s, KRYLOV - 1 : KRYLOV, :]
    tgt[q, 0:3, :] = centroids[...]
    tgt[q, 3:4, :] = weight[...]
    load_basis(basis, bmat)
    bmat_t[...] = bmat[...].T
    gram_high, gram_low = gram(bmat[...])
    for k in range(PLANE):
        gram_out[k, 0:1, :] = gram_high[k : k + 1]
        gram_out[k, 1:2, :] = gram_low[k : k + 1]

    pl.semaphore_wait(barrier, DEPTH + PLANE - 2)

    def to_slot(i, sem):
        send(src.at[own_slot], src.at[lax.rem(i + own_slot, DEPTH)], sem, on_line(i))

    @pl.loop(1, 5)
    def _(i):
        to_slot(i, 0)

    @pl.loop(13, DEPTH)
    def _(i):
        to_slot(i, 0)

    to_plane(tgt, 2)

    @pl.loop(5, 13)
    def _(i):
        to_slot(i, 1)

    gram_in[q] = gram_out[q]

    @pl.loop(1, PLANE)
    def _(i):
        to = lax.rem(q + i, PLANE)
        send(gram_out.at[to], gram_in.at[q], 3, on_plane(to))

    def prepare(slots):
        for b in slots:
            block = src[b]
            pieces = pieces_of(block, block[3:4] * CORE)
            rows = slice(b * SEG, (b + 1) * SEG)
            feat[rows, :] = contract(pieces, source_sel[...], (0, 1)).astype(bf16)
            scaled = block[4:8] * (block[3:4] * (1.0 / PANELS**0.5))
            high = rounded(scaled)
            vecs[:, rows] = jnp.concatenate(
                [high, scaled - high, jnp.zeros((8, SEG), f32)], axis=0
            ).astype(bf16)

    def operate(meets, total, slots):
        for b in range(slots[0] // 2, slots[1] // 2):
            rows = slice(b * CHUNK, (b + 1) * CHUNK)
            entry = lax.rsqrt(contract(feat[rows, :], meets, (1, 0)))
            high = entry.astype(bf16)
            low = (entry - high.astype(f32)).astype(bf16)
            total = total + contract(vecs[:, rows], high, (1, 0))
            total = total + contract(vecs[:, rows], low, (1, 0))
        return total

    settle(src, NEAR - 1, recv_sem.at[0])
    prepare(range(NEAR))
    settle(tgt, PLANE - 1, recv_sem.at[2])

    @pl.loop(0, ROWS)
    def _(i):
        pieces = []
        for core in range(2):
            block = jnp.concatenate([tgt[2 * i + core], jnp.zeros((4, SEG), f32)], axis=0)
            pieces.append(pieces_of(block, 0.0))
        meets = contract(target_sel[...], jnp.concatenate(pieces, axis=1), (1, 0)).astype(bf16)
        meet[i] = meets
        sums[i] = operate(meets, jnp.zeros((16, CHUNK), f32), (0, NEAR))

    def collect(buf, count):
        return fold([(buf[i, 0:1, :], buf[i, 1:2, :]) for i in range(count)])

    settle(gram_in, PLANE - 1, recv_sem.at[3])
    high, low = collect(gram_in, PLANE)
    gram_z[z, 0:1, :] = high
    gram_z[z, 1:2, :] = low
    to_line(gram_z, 4)

    settle(src, DEPTH - NEAR, recv_sem.at[1])
    prepare(range(NEAR, DEPTH))

    def away(i):
        return lax.rem(2 + i * (i + 1) // 2, 4)

    @pl.loop(0, ROWS)
    def _(i):
        x = lax.rem(r // 4 + away(i // 4), 4)
        y = lax.rem(lax.rem(r, 4) + away(lax.rem(i, 4)), 4)
        other = 4 * x + y
        total = operate(meet[other], sums[other], (NEAR, DEPTH))
        total = total[0:4] + total[4:8]
        for core in range(2):
            to = 2 * other + core
            mine = total[:, core * SEG : (core + 1) * SEG]

            @pl.when(to == q)
            def _():
                landed[q] = mine

            @pl.when(to != q)
            def _():
                part[to] = mine
                send(part.at[to], landed.at[q], 6, on_plane(to))

    settle(gram_z, DEPTH - 1, recv_sem.at[4])
    high, low = collect(gram_z, DEPTH)
    gram_all[q, 0:1, :] = high
    gram_all[q, 1:2, :] = low
    to_plane(gram_all, 5)

    settle(landed, PLANE - 1, recv_sem.at[6])
    applied = jnp.sum(landed[...], axis=0)

    high, low = payload(applied, bmat_t[...])
    dots_z[z, 0:1, :] = high
    dots_z[z, 1:2, :] = low
    to_line(dots_z, 7)
    settle(dots_z, DEPTH - 1, recv_sem.at[7])
    high, low = collect(dots_z, DEPTH)
    dots_q[q, 0:1, :] = high
    dots_q[q, 1:2, :] = low
    to_plane(dots_q, 8)
    settle(gram_all, PLANE - 1, recv_sem.at[5])
    gram_high = jnp.concatenate([gram_all[k, 0:1, :] for k in range(PLANE)], axis=0)
    gram_low = jnp.concatenate([gram_all[k, 1:2, :] for k in range(PLANE)], axis=0)
    settle(dots_q, PLANE - 1, recv_sem.at[8])
    vector, column = finish(applied, collect(dots_q, PLANE), (gram_high, gram_low), bmat[...])
    new_vector[...] = vector
    for s in range(SYSTEMS):
        hessenberg[s : s + 1, :] = column[:, 32 * s : 32 * s + KRYLOV + 1]

    settle(src, NEAR - 1, send_sem.at[0])
    settle(src, DEPTH - NEAR, send_sem.at[1])
    settle(tgt, PLANE - 1, send_sem.at[2])
    settle(gram_in, PLANE - 1, send_sem.at[3])
    settle(gram_z, DEPTH - 1, send_sem.at[4])
    settle(gram_all, PLANE - 1, send_sem.at[5])
    settle(landed, PLANE - 1, send_sem.at[6])
    settle(dots_z, DEPTH - 1, send_sem.at[7])
    settle(dots_q, PLANE - 1, send_sem.at[8])

def per_device(centroids, weight, basis):
    source, target = selections()
    vmem = pl.BlockSpec(memory_space=pltpu.VMEM)
    return pl.pallas_call(
        step_kernel,
        out_shape=(
            jax.ShapeDtypeStruct((SYSTEMS, SEG), f32),
            jax.ShapeDtypeStruct((SYSTEMS, KRYLOV + 1), f32),
        ),
        in_specs=[vmem] * 5,
        out_specs=(vmem, vmem),
        scratch_shapes=[
            pltpu.VMEM((DEPTH, 8, SEG), f32),
            pltpu.VMEM((PLANE, 4, SEG), f32),
            pltpu.VMEM((SOURCES, FEATURES), bf16),
            pltpu.VMEM((ROWS, FEATURES, CHUNK), bf16),
            pltpu.VMEM((16, SOURCES), bf16),
            pltpu.VMEM((ROWS, 16, CHUNK), f32),
            pltpu.VMEM((PLANE, 4, SEG), f32),
            pltpu.VMEM((PLANE, 4, SEG), f32),
            pltpu.VMEM((SEG, SEG), f32),
            pltpu.VMEM((SEG, SEG), f32),
            pltpu.VMEM((PLANE, 2, SEG), f32),
            pltpu.VMEM((PLANE, 2, SEG), f32),
            pltpu.VMEM((DEPTH, 2, SEG), f32),
            pltpu.VMEM((PLANE, 2, SEG), f32),
            pltpu.VMEM((DEPTH, 2, SEG), f32),
            pltpu.VMEM((PLANE, 2, SEG), f32),
            pltpu.SemaphoreType.DMA((9,)),
            pltpu.SemaphoreType.DMA((9,)),
        ],
        compiler_params=pltpu.CompilerParams(
            collective_id=0, has_side_effects=True, vmem_limit_bytes=40 * 2**20
        ),
        name="arnoldi_step",
    )(centroids, weight.reshape(1, SEG), basis, jnp.asarray(source, bf16), jnp.asarray(target, bf16))


def solution(mesh):
    placed = (P(None, ("col", "row")), P(("col", "row")), P(None, None, ("col", "row")))
    return jax.shard_map(
        per_device,
        mesh=mesh,
        in_specs=placed,
        out_specs=(P(None, ("col", "row")), P()),
        check_vma=False,
    )
```

time: 83.1 us -> 62.2 us (0.75)
  Pallas kernels: 80.2 us -> 59.3 us
    pallas_call x1, Pallas kernels: 80.2 us -> 59.3 us  [per_device(): pl.pallas_call(step_kernel, out_shape=(jax.ShapeDtypeStruct((SYSTEMS, SEG...]
where the time goes in v2:
time: 62.2 us; the launch traced here: 62 us
  Pallas kernels  59.3 us (95%)
  local copies, waits for them, and re-layouts  2.04 us (3%)
  between operations  0.69 us (1%)
    pallas_call x1, Pallas kernels, per_device(): pl.pallas_call(step_kernel, out_shape=(jax.ShapeDtypeStruct((SYSTEMS, SEG...  59.3 us
    unnamed x11, local copies, waits for them, and re-layouts  2.04 us

profile of v2, /device:TPU:1, one launch (start us, length us, event | category | flops | bytes accessed | tf_op | source)
XLA Modules:
  0.0 62.0 jit_solution(11406354763385341035)
XLA Ops:
  0.6 0.0 copy-start
  0.6 0.0 copy-start.1
  0.7 0.0 copy-start.2
  0.7 0.0 copy-start.3
  0.7 0.9 %copy.7.basis = f32[4,30,128]{2,1,0:T(8,128)S(1)} copy(f32[4,30,128]{2,0,1:T(4,128)} %param.7) | data formatting | bytes 122880 | tf_op args[2]
  1.5 0.0 copy-done
  1.5 0.0 copy-done.1
  1.5 0.0 copy-done.2
  1.5 0.0 copy-done.3
  1.6 59.3 %arnoldi_step.1 = (f32[4,128]{1,0:T(4,128)S(1)}, f32[4,31]{1,0:T(4,128)S(1)}) custom-call(f32[3,128]{1,0:T(4,128)S(1)} %copy-done.2, f32[1,128]{1,0:T(1,128)S(1)} %bitcast.1, f32[4,30,128]{2,1,0:T(8,128)S(1)} %copy.7.basis, bf16[128,48]{1,0:T(8,128)(2,1)S(1)} %copy-done.1, bf16[128,48]{1,0:T(8,128)(2,1)S(1)} %copy-done), custom_call_target="tpu_custom_call" | custom-call | tf_op jit(solution)/shard_map/arnoldi_step/pallas_call | solution.py:453
  60.9 0.6 copy.10
  61.4 0.6 copy.11
Async XLA Ops:
  0.6 0.9 %copy-start = (bf16[128,48]{1,0:T(8,128)(2,1)S(1)}, bf16[128,48]{1,0:T(8,128)(2,1)}, u32[]{:S(2)}) copy-start(bf16[128,48]{1,0:T(8,128)(2,1)} %constant.5.clone.target_sel) | copy-start | bytes 36868
  0.6 0.9 %copy-start.1 = (bf16[128,48]{1,0:T(8,128)(2,1)S(1)}, bf16[128,48]{1,0:T(8,128)(2,1)}, u32[]{:S(2)}) copy-start(bf16[128,48]{1,0:T(8,128)(2,1)} %constant.4.clone.source_sel) | copy-start | bytes 36868
  0.7 0.9 %copy-start.2 = (f32[3,128]{1,0:T(4,128)S(1)}, f32[3,128]{1,0:T(4,128)}, u32[]{:S(2)}) copy-start(f32[3,128]{1,0:T(4,128)} %centroids.1) | copy-start | bytes 4612
  0.7 0.9 %copy-start.3 = (f32[128]{0:T(128)S(1)}, f32[128]{0:T(128)}, u32[]{:S(2)}) copy-start(f32[128]{0:T(128)} %param.6) | copy-start | bytes 1540

commit v3 on v2

--- a/solution.py
+++ b/solution.py
@@ -25,9 +25,13 @@
 DEPTH = 16
 PLANE = 32
 NEAR = 8
-DEPTH = 16
-PLANE = 32
-NEAR = 8
+REACH = 4
+OUTWARD = (
+    ((2, 2), (3, 2), (3, 3), (3, 0)),
+    ((2, 1), (1, 1), (2, 0), (0, 1)),
+    ((2, 3), (1, 3), (0, 2), (0, 3)),
+    ((1, 2), (3, 1), (1, 0), (0, 0)),
+)
 EPSILON = 1e-06
 
 
@@ -87,86 +91,6 @@
 
 def contract(a, b, dims, **kw):
     return lax.dot_general(a, b, ((dims[:1], dims[1:]), ((), ())), preferred_element_type=f32, **kw)
-
-
-def two_sum(a,b):
-    s=a+b
-    t=s-a
-    return s,(a-(s-t))+(b-t)
-def pair_sum(p,q):
-    s,e=two_sum(p[0],q[0])
-    e=e+(p[1]+q[1])
-    h=s+e
-    return h,e-(h-s)
-def pair_product(a,b):
-    p=a*b
-    ah,bh=rounded(a),rounded(b)
-    al,bl=a-ah,b-bh
-    return p,((ah*bh-p)+ah*bl+al*bh)+al*bl
-def fold(parts):
-    while len(parts)>1:
-        parts=[pair_sum(*parts[i:i+2]) if i+1<len(parts) else parts[i] for i in range(0,len(parts),2)]
-    return parts[0]
-def down(p):
-    m=p[0].shape[0]//8
-    p=fold([(p[0][8*i:8*i+8],p[1][8*i:8*i+8]) for i in range(m)])
-    for by in (4,2,1):
-        p=pair_sum(p,(pltpu.roll(p[0],by,0),pltpu.roll(p[1],by,0)))
-    return p[0][0:1],p[1][0:1]
-def across(by_row):
-    lane=lax.broadcasted_iota(jnp.int32,(32,SEG),1)//32
-    out=by_row[0:32]
-    for s in range(1,SYSTEMS):
-        out=jnp.where(lane==s,by_row[32*s:32*s+32],out)
-    return out
-def gram(b):
-    slices=[]
-    rest=b
-    for bits in (4,12,20,28):
-        q=jnp.floor(rest*2.0**bits+0.5)*2.0**-bits
-        rest=rest-q
-        slices.append(q.astype(bf16))
-    total=None
-    for level in range(5):
-        pairs=[(i,level-i) for i in range(4) if 0<=level-i<4]
-        left=jnp.concatenate([slices[i] for i,_ in pairs],axis=1)
-        right=jnp.concatenate([slices[j] for _,j in pairs],axis=1)
-        part=across(contract(left,right,(1,1)))
-        exact=(part,jnp.zeros_like(part))
-        total=exact if total is None else pair_sum(total,exact)
-    return total[0]*(1.0/PANELS),total[1]*(1.0/PANELS)
-def payload(a,bt):
-    lane=lax.broadcasted_iota(jnp.int32,(SEG,SEG),1)%32
-    at=jnp.concatenate([jnp.broadcast_to(a[s:s+1],(32,SEG)) for s in range(SYSTEMS)],axis=0).T
-    h,l=down(pair_product(at,jnp.where(lane==KRYLOV,at,bt)))
-    return h*(1.0 / PANELS),l*(1.0 / PANELS)
-def finish(a,p,g,bmat):
-    k=lax.broadcasted_iota(jnp.int32,(1,SEG),1)%32
-    system=lax.broadcasted_iota(jnp.int32,(8,SEG),0)
-    lane=lax.broadcasted_iota(jnp.int32,(8,SEG),1)
-    own=lane//32==system
-    def times(c):
-        column=across(jnp.broadcast_to(c,(SEG,SEG)).T)
-        h,l=pair_product(g[0],column)
-        return down((h,l+g[1]*column))
-    basis_lane=k<KRYLOV
-    fh,fl=jnp.where(basis_lane,p[0],0.0),jnp.where(basis_lane,p[1],0.0)
-    gf=times(fh)
-    second=(fh-gf[0])+(fl-gf[1])
-    c=fh+second
-    a8=jnp.concatenate([a,jnp.zeros((4,SEG),f32)],axis=0)
-    twice=a8-contract(jnp.where(own,jnp.broadcast_to(c,(8,SEG)),0.0),bmat,(1,0),precision=HIGHEST)
-    gc=times(c)
-    u=pair_sum(gc,(-2.0*fh,-2.0*fl))
-    h,l=pair_product(c,u[0])
-    l=l+c*u[1]
-    square=(jnp.where(k==KRYLOV,p[0],h),jnp.where(k==KRYLOV,p[1],l))
-    for by in (1,2,4,8,16):
-        square=pair_sum(square,(pltpu.roll(square[0],by,1),pltpu.roll(square[1],by,1)))
-    length=jnp.sqrt(jnp.maximum(square[0]+square[1],0.0)+EPSILON)
-    each=jnp.sum(jnp.where(own&(lane%32==31),jnp.broadcast_to(length,(8,SEG)),0.0),axis=1,keepdims=True)
-    new=(twice/jnp.where(system[:,0:1]<SYSTEMS,each,1.0))[0:SYSTEMS]
-    return new,jnp.where(k==KRYLOV,pltpu.roll(length,SEG-1,1),c)
 
 
 def load_basis(basis,bmat):
@@ -267,11 +191,16 @@
     def on_plane(to):
         return to // 2, 2 * z + lax.rem(to, 2)
 
+    def near_offset(i):
+        return lax.rem(DEPTH - REACH - 1 + i + lax.select(i > REACH, 1, 0), DEPTH)
+
     barrier = pltpu.get_barrier_semaphore()
 
-    @pl.loop(1, DEPTH)
+    @pl.loop(1, 2 * REACH + 1)
     def _(i):
-        pl.semaphore_signal(barrier, inc=1, device_id=on_line(i), device_id_type=MESH)
+        pl.semaphore_signal(
+            barrier, inc=1, device_id=on_line(near_offset(i)), device_id_type=MESH
+        )
 
     @pl.loop(1, PLANE)
     def _(i):
@@ -313,24 +242,17 @@
         gram_out[k, 0:1, :] = gram_high[k : k + 1]
         gram_out[k, 1:2, :] = gram_low[k : k + 1]
 
-    pl.semaphore_wait(barrier, DEPTH + PLANE - 2)
+    pl.semaphore_wait(barrier, 2 * REACH + PLANE - 1)
 
     def to_slot(i, sem):
         send(src.at[own_slot], src.at[lax.rem(i + own_slot, DEPTH)], sem, on_line(i))
 
-    @pl.loop(1, 5)
+    @pl.loop(2, 2 * REACH + 1)
     def _(i):
-        to_slot(i, 0)
-
-    @pl.loop(13, DEPTH)
-    def _(i):
-        to_slot(i, 0)
+        to_slot(near_offset(i), 0)
 
     to_plane(tgt, 2)
-
-    @pl.loop(5, 13)
-    def _(i):
-        to_slot(i, 1)
+    to_slot(DEPTH - REACH, 1)
 
     gram_in[q] = gram_out[q]
 
@@ -362,18 +284,35 @@
         return total
 
     settle(src, NEAR - 1, recv_sem.at[0])
+    ahead, behind = REACH, REACH - 1
+    send(
+        src.at[pl.ds(own_slot + 1, ahead)], src.at[pl.ds(own_slot + 1 + REACH, ahead)],
+        1, on_line(REACH),
+    )
+    send(
+        src.at[pl.ds(own_slot - behind, behind)],
+        src.at[pl.ds(DEPTH - 1 - behind, behind)],
+        1, on_line(DEPTH - REACH),
+    )
     prepare(range(NEAR))
     settle(tgt, PLANE - 1, recv_sem.at[2])
 
-    @pl.loop(0, ROWS)
-    def _(i):
-        pieces = []
-        for core in range(2):
-            block = jnp.concatenate([tgt[2 * i + core], jnp.zeros((4, SEG), f32)], axis=0)
-            pieces.append(pieces_of(block, 0.0))
-        meets = contract(target_sel[...], jnp.concatenate(pieces, axis=1), (1, 0)).astype(bf16)
-        meet[i] = meets
-        sums[i] = operate(meets, jnp.zeros((16, CHUNK), f32), (0, NEAR))
+    @pl.loop(0, ROWS // 4)
+    def _(step):
+        for i in range(4):
+            pieces = []
+            for core in range(2):
+                block = tgt[2 * (4 * step + i) + core]
+                block = jnp.concatenate([block, jnp.zeros((4, SEG), f32)], axis=0)
+                pieces.append(pieces_of(block, 0.0))
+            pieces = jnp.concatenate(pieces, axis=1)
+            meet[4 * step + i] = contract(target_sel[...], pieces, (1, 0)).astype(bf16)
+
+    @pl.loop(0, ROWS // 4)
+    def _(step):
+        for i in range(4):
+            at = 4 * step + i
+            sums[at] = operate(meet[at], jnp.zeros((16, CHUNK), f32), (0, NEAR))
 
     def collect(buf, count):
         return fold([(buf[i, 0:1, :], buf[i, 1:2, :]) for i in range(count)])
@@ -387,42 +326,46 @@
     settle(src, DEPTH - NEAR, recv_sem.at[1])
     prepare(range(NEAR, DEPTH))
 
-    def away(i):
-        return lax.rem(2 + i * (i + 1) // 2, 4)
-
-    @pl.loop(0, ROWS)
-    def _(i):
-        x = lax.rem(r // 4 + away(i // 4), 4)
-        y = lax.rem(lax.rem(r, 4) + away(lax.rem(i, 4)), 4)
-        other = 4 * x + y
-        total = operate(meet[other], sums[other], (NEAR, DEPTH))
-        total = total[0:4] + total[4:8]
-        for core in range(2):
-            to = 2 * other + core
-            mine = total[:, core * SEG : (core + 1) * SEG]
-
-            @pl.when(to == q)
-            def _():
-                landed[q] = mine
-
-            @pl.when(to != q)
-            def _():
-                part[to] = mine
-                send(part.at[to], landed.at[q], 6, on_plane(to))
-
+    def chosen(step, options):
+        value = options[-1]
+        for at in range(len(options) - 1):
+            value = lax.select(step == at, options[at], value)
+        return value
+
+    def other_chip(step, i):
+        x = lax.rem(r // 4 + chosen(step, [pair[0] for pair in OUTWARD[i]]), 4)
+        y = lax.rem(lax.rem(r, 4) + chosen(step, [pair[1] for pair in OUTWARD[i]]), 4)
+        return 4 * x + y
+
+    @pl.loop(0, ROWS // 4)
+    def _(step):
+        for i in range(4):
+            other = other_chip(step, i)
+            total = operate(meet[other], sums[other], (NEAR, DEPTH))
+            total = total[0:4] + total[4:8]
+            part[2 * other] = total[:, 0:SEG]
+            part[2 * other + 1] = total[:, SEG:CHUNK]
+        for i in range(4):
+            for core in range(2):
+                to = 2 * other_chip(step, i) + core
+
+                @pl.when(to != q)
+                def _():
+                    send(part.at[to], landed.at[q], 6, on_plane(to))
+
+    landed[q] = part[q]
+    settle(landed, PLANE - 1, recv_sem.at[6])
+    applied = jnp.sum(landed[...], axis=0)
+
+    high, low = payload(applied, bmat_t[...])
+    dots_z[z, 0:1, :] = high
+    dots_z[z, 1:2, :] = low
+    to_line(dots_z, 7)
     settle(gram_z, DEPTH - 1, recv_sem.at[4])
     high, low = collect(gram_z, DEPTH)
     gram_all[q, 0:1, :] = high
     gram_all[q, 1:2, :] = low
     to_plane(gram_all, 5)
-
-    settle(landed, PLANE - 1, recv_sem.at[6])
-    applied = jnp.sum(landed[...], axis=0)
-
-    high, low = payload(applied, bmat_t[...])
-    dots_z[z, 0:1, :] = high
-    dots_z[z, 1:2, :] = low
-    to_line(dots_z, 7)
     settle(dots_z, DEPTH - 1, recv_sem.at[7])
     high, low = collect(dots_z, DEPTH)
     dots_q[q, 0:1, :] = high

time: 62.2 us -> 52.9 us (0.85)
  Pallas kernels: 59.3 us -> 50 us
    pallas_call x1, Pallas kernels: 59.3 us -> 50 us  [per_device(): pl.pallas_call(step_kernel, out_shape=(jax.ShapeDtypeStruct((SYSTEMS, SEG...]
where the time goes in v3:
time: 52.9 us; the launch traced here: 52.7 us
  Pallas kernels  50 us (95%)
  local copies, waits for them, and re-layouts  2.04 us (4%)
  between operations  0.69 us (1%)
    pallas_call x1, Pallas kernels, per_device(): pl.pallas_call(step_kernel, out_shape=(jax.ShapeDtypeStruct((SYSTEMS, SEG...  50 us
    unnamed x11, local copies, waits for them, and re-layouts  2.04 us

profile of v3, /device:TPU:1, one launch (start us, length us, event | category | flops | bytes accessed | tf_op | source)
XLA Modules:
  0.0 52.7 jit_solution(15601483372333882795)
XLA Ops:
  0.6 0.0 copy-start
  0.6 0.0 copy-start.1
  0.7 0.0 copy-start.2
  0.7 0.0 copy-start.3
  0.7 0.9 %copy.7.basis = f32[4,30,128]{2,1,0:T(8,128)S(1)} copy(f32[4,30,128]{2,0,1:T(4,128)} %param.7) | data formatting | bytes 122880 | tf_op args[2]
  1.5 0.0 copy-done
  1.5 0.0 copy-done.1
  1.5 0.0 copy-done.2
  1.5 0.0 copy-done.3
  1.6 50.0 %arnoldi_step.1 = (f32[4,128]{1,0:T(4,128)S(1)}, f32[4,31]{1,0:T(4,128)S(1)}) custom-call(f32[3,128]{1,0:T(4,128)S(1)} %copy-done.2, f32[1,128]{1,0:T(1,128)S(1)} %bitcast.1, f32[4,30,128]{2,1,0:T(8,128)S(1)} %copy.7.basis, bf16[128,48]{1,0:T(8,128)(2,1)S(1)} %copy-done.1, bf16[128,48]{1,0:T(8,128)(2,1)S(1)} %copy-done), custom_call_target="tpu_custom_call" | custom-call | tf_op jit(solution)/shard_map/arnoldi_step/pallas_call | solution.py:396
  51.5 0.6 %copy.10 = f32[4,128]{1,0:T(4,128)} copy(f32[4,128]{1,0:T(4,128)S(1)} %get-tuple-element.4) | data formatting | bytes 4096
  52.1 0.6 %copy.11 = f32[4,31]{1,0:T(4,128)} copy(f32[4,31]{1,0:T(4,128)S(1)} %get-tuple-element.5) | data formatting | bytes 992
Async XLA Ops:
  0.6 0.9 %copy-start = (bf16[128,48]{1,0:T(8,128)(2,1)S(1)}, bf16[128,48]{1,0:T(8,128)(2,1)}, u32[]{:S(2)}) copy-start(bf16[128,48]{1,0:T(8,128)(2,1)} %constant.5.clone.target_sel) | copy-start | bytes 36868
  0.6 0.9 %copy-start.1 = (bf16[128,48]{1,0:T(8,128)(2,1)S(1)}, bf16[128,48]{1,0:T(8,128)(2,1)}, u32[]{:S(2)}) copy-start(bf16[128,48]{1,0:T(8,128)(2,1)} %constant.4.clone.source_sel) | copy-start | bytes 36868
  0.7 0.9 %copy-start.2 = (f32[3,128]{1,0:T(4,128)S(1)}, f32[3,128]{1,0:T(4,128)}, u32[]{:S(2)}) copy-start(f32[3,128]{1,0:T(4,128)} %centroids.1) | copy-start | bytes 4612
  0.7 0.9 %copy-start.3 = (f32[128]{0:T(128)S(1)}, f32[128]{0:T(128)}, u32[]{:S(2)}) copy-start(f32[128]{0:T(128)} %param.6) | copy-start | bytes 1540

commit v4 on v3

--- a/solution.py
+++ b/solution.py
@@ -27,10 +27,8 @@
 NEAR = 8
 REACH = 4
 OUTWARD = (
-    ((2, 2), (3, 2), (3, 3), (3, 0)),
-    ((2, 1), (1, 1), (2, 0), (0, 1)),
-    ((2, 3), (1, 3), (0, 2), (0, 3)),
-    ((1, 2), (3, 1), (1, 0), (0, 0)),
+    (2, 2), (2, 1), (2, 3), (1, 2), (3, 2), (1, 1), (1, 3), (3, 1),
+    (3, 3), (2, 0), (0, 2), (1, 0), (3, 0), (0, 1), (0, 3), (0, 0),
 )
 EPSILON = 1e-06
 
@@ -235,25 +233,25 @@
         src[own_slot, 4 + s : 5 + s, :] = basis[s, KRYLOV - 1 : KRYLOV, :]
     tgt[q, 0:3, :] = centroids[...]
     tgt[q, 3:4, :] = weight[...]
+
+    pl.semaphore_wait(barrier, 2 * REACH + PLANE - 1)
+
+    def to_slot(i, sem):
+        send(src.at[own_slot], src.at[lax.rem(i + own_slot, DEPTH)], sem, on_line(i))
+
+    @pl.loop(2, 2 * REACH + 1)
+    def _(i):
+        to_slot(near_offset(i), 0)
+
+    to_plane(tgt, 2)
+    to_slot(DEPTH - REACH, 1)
+
     load_basis(basis, bmat)
     bmat_t[...] = bmat[...].T
     gram_high, gram_low = gram(bmat[...])
     for k in range(PLANE):
         gram_out[k, 0:1, :] = gram_high[k : k + 1]
         gram_out[k, 1:2, :] = gram_low[k : k + 1]
-
-    pl.semaphore_wait(barrier, 2 * REACH + PLANE - 1)
-
-    def to_slot(i, sem):
-        send(src.at[own_slot], src.at[lax.rem(i + own_slot, DEPTH)], sem, on_line(i))
-
-    @pl.loop(2, 2 * REACH + 1)
-    def _(i):
-        to_slot(near_offset(i), 0)
-
-    to_plane(tgt, 2)
-    to_slot(DEPTH - REACH, 1)
-
     gram_in[q] = gram_out[q]
 
     @pl.loop(1, PLANE)
@@ -297,63 +295,71 @@
     prepare(range(NEAR))
     settle(tgt, PLANE - 1, recv_sem.at[2])
 
+    def other_chip(shift):
+        return 4 * lax.rem(r // 4 + shift[0], 4) + lax.rem(lax.rem(r, 4) + shift[1], 4)
+
+    def chosen(step, options):
+        value = options[-1]
+        for at in range(len(options) - 1):
+            value = lax.select(step == at, options[at], value)
+        return value
+
     @pl.loop(0, ROWS // 4)
     def _(step):
         for i in range(4):
+            shift = [chosen(step, [pair[axis] for pair in OUTWARD[i::4]]) for axis in range(2)]
+            other = other_chip(shift)
             pieces = []
             for core in range(2):
-                block = tgt[2 * (4 * step + i) + core]
-                block = jnp.concatenate([block, jnp.zeros((4, SEG), f32)], axis=0)
+                block = jnp.concatenate([tgt[2 * other + core], jnp.zeros((4, SEG), f32)], axis=0)
                 pieces.append(pieces_of(block, 0.0))
             pieces = jnp.concatenate(pieces, axis=1)
             meet[4 * step + i] = contract(target_sel[...], pieces, (1, 0)).astype(bf16)
 
-    @pl.loop(0, ROWS // 4)
+    nothing = jnp.zeros((16, CHUNK), f32)
+
+    @pl.loop(0, (ROWS - 1) // 5)
     def _(step):
-        for i in range(4):
-            at = 4 * step + i
-            sums[at] = operate(meet[at], jnp.zeros((16, CHUNK), f32), (0, NEAR))
+        for i in range(5):
+            at = 5 * step + i
+            sums[at] = operate(meet[at], nothing, (0, NEAR))
 
     def collect(buf, count):
         return fold([(buf[i, 0:1, :], buf[i, 1:2, :]) for i in range(count)])
 
+    settle(src, DEPTH - NEAR, recv_sem.at[1])
+    prepare(range(NEAR, DEPTH))
+
+    def finished(at, other):
+        total = operate(meet[at], sums[at], (NEAR, DEPTH))
+        total = total[0:4] + total[4:8]
+        part[2 * other] = total[:, 0:SEG]
+        part[2 * other + 1] = total[:, SEG:CHUNK]
+
+    def deliver(to):
+        send(part.at[to], landed.at[q], 6, on_plane(to))
+
+    @pl.loop(0, (ROWS - 1) // 5)
+    def _(step):
+        others = []
+        for i in range(5):
+            shifts = OUTWARD[i : ROWS - 1 : 5]
+            others.append(other_chip([chosen(step, [p[axis] for p in shifts]) for axis in range(2)]))
+            finished(5 * step + i, others[-1])
+        for other in others:
+            deliver(2 * other)
+            deliver(2 * other + 1)
+
+    sums[ROWS - 1] = operate(meet[ROWS - 1], nothing, (0, NEAR))
+    finished(ROWS - 1, r)
+    deliver(2 * r + 1 - lax.rem(c, 2))
+    landed[q] = part[q]
     settle(gram_in, PLANE - 1, recv_sem.at[3])
     high, low = collect(gram_in, PLANE)
     gram_z[z, 0:1, :] = high
     gram_z[z, 1:2, :] = low
     to_line(gram_z, 4)
 
-    settle(src, DEPTH - NEAR, recv_sem.at[1])
-    prepare(range(NEAR, DEPTH))
-
-    def chosen(step, options):
-        value = options[-1]
-        for at in range(len(options) - 1):
-            value = lax.select(step == at, options[at], value)
-        return value
-
-    def other_chip(step, i):
-        x = lax.rem(r // 4 + chosen(step, [pair[0] for pair in OUTWARD[i]]), 4)
-        y = lax.rem(lax.rem(r, 4) + chosen(step, [pair[1] for pair in OUTWARD[i]]), 4)
-        return 4 * x + y
-
-    @pl.loop(0, ROWS // 4)
-    def _(step):
-        for i in range(4):
-            other = other_chip(step, i)
-            total = operate(meet[other], sums[other], (NEAR, DEPTH))
-            total = total[0:4] + total[4:8]
-            part[2 * other] = total[:, 0:SEG]
-            part[2 * other + 1] = total[:, SEG:CHUNK]
-        for i in range(4):
-            for core in range(2):
-                to = 2 * other_chip(step, i) + core
-
-                @pl.when(to != q)
-                def _():
-                    send(part.at[to], landed.at[q], 6, on_plane(to))
-
-    landed[q] = part[q]
     settle(landed, PLANE - 1, recv_sem.at[6])
     applied = jnp.sum(landed[...], axis=0)
 

time: 52.9 us -> 51.4 us (0.972)
  Pallas kernels: 50 us -> 48.5 us
    pallas_call x1, Pallas kernels: 50 us -> 48.5 us  [per_device(): pl.pallas_call(step_kernel, out_shape=(jax.ShapeDtypeStruct((SYSTEMS, SEG...]
where the time goes in v4:
time: 51.4 us; the launch traced here: 51.3 us
  Pallas kernels  48.5 us (94%)
  local copies, waits for them, and re-layouts  2.04 us (4%)
  between operations  0.69 us (1%)
    pallas_call x1, Pallas kernels, per_device(): pl.pallas_call(step_kernel, out_shape=(jax.ShapeDtypeStruct((SYSTEMS, SEG...  48.5 us
    unnamed x11, local copies, waits for them, and re-layouts  2.04 us

profile of v4, /device:TPU:1, one launch (start us, length us, event | category | flops | bytes accessed | tf_op | source)
XLA Modules:
  0.0 51.3 jit_solution(3591617019407703586)
XLA Ops:
  0.6 0.0 copy-start
  0.6 0.0 copy-start.1
  0.7 0.0 copy-start.2
  0.7 0.0 copy-start.3
  0.7 0.9 %copy.7.basis = f32[4,30,128]{2,1,0:T(8,128)S(1)} copy(f32[4,30,128]{2,0,1:T(4,128)} %param.7) | data formatting | bytes 122880 | tf_op args[2]
  1.5 0.0 copy-done
  1.5 0.0 copy-done.1
  1.5 0.0 copy-done.2
  1.5 0.0 copy-done.3
  1.6 48.5 %arnoldi_step.1 = (f32[4,128]{1,0:T(4,128)S(1)}, f32[4,31]{1,0:T(4,128)S(1)}) custom-call(f32[3,128]{1,0:T(4,128)S(1)} %copy-done.2, f32[1,128]{1,0:T(1,128)S(1)} %bitcast.1, f32[4,30,128]{2,1,0:T(8,128)S(1)} %copy.7.basis, bf16[128,48]{1,0:T(8,128)(2,1)S(1)} %copy-done.1, bf16[128,48]{1,0:T(8,128)(2,1)S(1)} %copy-done), custom_call_target="tpu_custom_call" | custom-call | tf_op jit(solution)/shard_map/arnoldi_step/pallas_call | solution.py:402
  50.1 0.6 %copy.10 = f32[4,128]{1,0:T(4,128)} copy(f32[4,128]{1,0:T(4,128)S(1)} %get-tuple-element.4) | data formatting | bytes 4096
  50.7 0.6 %copy.11 = f32[4,31]{1,0:T(4,128)} copy(f32[4,31]{1,0:T(4,128)S(1)} %get-tuple-element.5) | data formatting | bytes 992
Async XLA Ops:
  0.6 0.9 %copy-start = (bf16[128,48]{1,0:T(8,128)(2,1)S(1)}, bf16[128,48]{1,0:T(8,128)(2,1)}, u32[]{:S(2)}) copy-start(bf16[128,48]{1,0:T(8,128)(2,1)} %constant.5.clone.target_sel) | copy-start | bytes 36868
  0.6 0.9 %copy-start.1 = (bf16[128,48]{1,0:T(8,128)(2,1)S(1)}, bf16[128,48]{1,0:T(8,128)(2,1)}, u32[]{:S(2)}) copy-start(bf16[128,48]{1,0:T(8,128)(2,1)} %constant.4.clone.source_sel) | copy-start | bytes 36868
  0.7 0.9 %copy-start.2 = (f32[3,128]{1,0:T(4,128)S(1)}, f32[3,128]{1,0:T(4,128)}, u32[]{:S(2)}) copy-start(f32[3,128]{1,0:T(4,128)} %centroids.1) | copy-start | bytes 4612
  0.7 0.9 %copy-start.3 = (f32[128]{0:T(128)S(1)}, f32[128]{0:T(128)}, u32[]{:S(2)}) copy-start(f32[128]{0:T(128)} %param.6) | copy-start | bytes 1540

commit v5 on v4

--- a/solution.py
+++ b/solution.py
@@ -304,25 +304,19 @@
             value = lax.select(step == at, options[at], value)
         return value
 
-    @pl.loop(0, ROWS // 4)
-    def _(step):
-        for i in range(4):
-            shift = [chosen(step, [pair[axis] for pair in OUTWARD[i::4]]) for axis in range(2)]
-            other = other_chip(shift)
-            pieces = []
-            for core in range(2):
-                block = jnp.concatenate([tgt[2 * other + core], jnp.zeros((4, SEG), f32)], axis=0)
-                pieces.append(pieces_of(block, 0.0))
-            pieces = jnp.concatenate(pieces, axis=1)
-            meet[4 * step + i] = contract(target_sel[...], pieces, (1, 0)).astype(bf16)
+    for at in range(ROWS):
+        other = other_chip(OUTWARD[at])
+        pieces = []
+        for core in range(2):
+            block = jnp.concatenate([tgt[2 * other + core], jnp.zeros((4, SEG), f32)], axis=0)
+            pieces.append(pieces_of(block, 0.0))
+        pieces = jnp.concatenate(pieces, axis=1)
+        meet[at] = contract(target_sel[...], pieces, (1, 0)).astype(bf16)
 
     nothing = jnp.zeros((16, CHUNK), f32)
 
-    @pl.loop(0, (ROWS - 1) // 5)
-    def _(step):
-        for i in range(5):
-            at = 5 * step + i
-            sums[at] = operate(meet[at], nothing, (0, NEAR))
+    for at in range(ROWS - 1):
+        sums[at] = operate(meet[at], nothing, (0, NEAR))
 
     def collect(buf, count):
         return fold([(buf[i, 0:1, :], buf[i, 1:2, :]) for i in range(count)])

time: 51.4 us -> 50.4 us (0.981)
  Pallas kernels: 48.5 us -> 47.5 us
    pallas_call x1, Pallas kernels: 48.5 us -> 47.5 us  [per_device(): pl.pallas_call(step_kernel, out_shape=(jax.ShapeDtypeStruct((SYSTEMS, SEG...]
where the time goes in v5:
time: 50.4 us; the launch traced here: 50.2 us
  Pallas kernels  47.5 us (94%)
  local copies, waits for them, and re-layouts  2.04 us (4%)
  between operations  0.69 us (1%)
    pallas_call x1, Pallas kernels, per_device(): pl.pallas_call(step_kernel, out_shape=(jax.ShapeDtypeStruct((SYSTEMS, SEG...  47.5 us
    unnamed x11, local copies, waits for them, and re-layouts  2.04 us

profile of v5, /device:TPU:1, one launch (start us, length us, event | category | flops | bytes accessed | tf_op | source)
XLA Modules:
  0.0 50.2 jit_solution(6465360675040194101)
XLA Ops:
  0.6 0.0 copy-start
  0.6 0.0 copy-start.1
  0.7 0.0 copy-start.2
  0.7 0.0 copy-start.3
  0.7 0.9 %copy.7.basis = f32[4,30,128]{2,1,0:T(8,128)S(1)} copy(f32[4,30,128]{2,0,1:T(4,128)} %param.7) | data formatting | bytes 122880 | tf_op args[2]
  1.5 0.0 copy-done
  1.5 0.0 copy-done.1
  1.5 0.0 copy-done.2
  1.5 0.0 copy-done.3
  1.6 47.5 %arnoldi_step.1 = (f32[4,128]{1,0:T(4,128)S(1)}, f32[4,31]{1,0:T(4,128)S(1)}) custom-call(f32[3,128]{1,0:T(4,128)S(1)} %copy-done.2, f32[1,128]{1,0:T(1,128)S(1)} %bitcast.1, f32[4,30,128]{2,1,0:T(8,128)S(1)} %copy.7.basis, bf16[128,48]{1,0:T(8,128)(2,1)S(1)} %copy-done.1, bf16[128,48]{1,0:T(8,128)(2,1)S(1)} %copy-done), custom_call_target="tpu_custom_call" | custom-call | tf_op jit(solution)/shard_map/arnoldi_step/pallas_call | solution.py:396
  49.1 0.6 %copy.10 = f32[4,128]{1,0:T(4,128)} copy(f32[4,128]{1,0:T(4,128)S(1)} %get-tuple-element.4) | data formatting | bytes 4096
  49.7 0.6 %copy.11 = f32[4,31]{1,0:T(4,128)} copy(f32[4,31]{1,0:T(4,128)S(1)} %get-tuple-element.5) | data formatting | bytes 992
Async XLA Ops:
  0.6 0.9 %copy-start = (bf16[128,48]{1,0:T(8,128)(2,1)S(1)}, bf16[128,48]{1,0:T(8,128)(2,1)}, u32[]{:S(2)}) copy-start(bf16[128,48]{1,0:T(8,128)(2,1)} %constant.5.clone.target_sel) | copy-start | bytes 36868
  0.6 0.9 %copy-start.1 = (bf16[128,48]{1,0:T(8,128)(2,1)S(1)}, bf16[128,48]{1,0:T(8,128)(2,1)}, u32[]{:S(2)}) copy-start(bf16[128,48]{1,0:T(8,128)(2,1)} %constant.4.clone.source_sel) | copy-start | bytes 36868
  0.7 0.9 %copy-start.2 = (f32[3,128]{1,0:T(4,128)S(1)}, f32[3,128]{1,0:T(4,128)}, u32[]{:S(2)}) copy-start(f32[3,128]{1,0:T(4,128)} %centroids.1) | copy-start | bytes 4612
  0.7 0.9 %copy-start.3 = (f32[128]{0:T(128)S(1)}, f32[128]{0:T(128)}, u32[]{:S(2)}) copy-start(f32[128]{0:T(128)} %param.6) | copy-start | bytes 1540

commit v6 on v5

--- a/solution.py
+++ b/solution.py
@@ -333,13 +333,10 @@
     def deliver(to):
         send(part.at[to], landed.at[q], 6, on_plane(to))
 
-    @pl.loop(0, (ROWS - 1) // 5)
-    def _(step):
-        others = []
-        for i in range(5):
-            shifts = OUTWARD[i : ROWS - 1 : 5]
-            others.append(other_chip([chosen(step, [p[axis] for p in shifts]) for axis in range(2)]))
-            finished(5 * step + i, others[-1])
+    for start in range(0, ROWS - 1, 8):
+        others = [other_chip(shift) for shift in OUTWARD[start : min(start + 8, ROWS - 1)]]
+        for i, other in enumerate(others):
+            finished(start + i, other)
         for other in others:
             deliver(2 * other)
             deliver(2 * other + 1)

time: 50.4 us -> 50.5 us (level)
  no operation moved by 1% of the time
where the time goes in v6:
time: 50.5 us; the launch traced here: 50.4 us
  Pallas kernels  47.6 us (94%)
  local copies, waits for them, and re-layouts  2.04 us (4%)
  between operations  0.69 us (1%)
    pallas_call x1, Pallas kernels, per_device(): pl.pallas_call(step_kernel, out_shape=(jax.ShapeDtypeStruct((SYSTEMS, SEG...  47.6 us
    unnamed x11, local copies, waits for them, and re-layouts  2.04 us

profile of v6, /device:TPU:1, one launch (start us, length us, event | category | flops | bytes accessed | tf_op | source)
XLA Modules:
  0.0 50.4 jit_solution(3803558163010176428)
XLA Ops:
  0.6 0.0 copy-start
  0.6 0.0 copy-start.1
  0.7 0.0 copy-start.2
  0.7 0.0 copy-start.3
  0.7 0.9 %copy.7.basis = f32[4,30,128]{2,1,0:T(8,128)S(1)} copy(f32[4,30,128]{2,0,1:T(4,128)} %param.7) | data formatting | bytes 122880 | tf_op args[2]
  1.5 0.0 copy-done
  1.5 0.0 copy-done.1
  1.5 0.0 copy-done.2
  1.5 0.0 copy-done.3
  1.6 47.6 %arnoldi_step.1 = (f32[4,128]{1,0:T(4,128)S(1)}, f32[4,31]{1,0:T(4,128)S(1)}) custom-call(f32[3,128]{1,0:T(4,128)S(1)} %copy-done.2, f32[1,128]{1,0:T(1,128)S(1)} %bitcast.1, f32[4,30,128]{2,1,0:T(8,128)S(1)} %copy.7.basis, bf16[128,48]{1,0:T(8,128)(2,1)S(1)} %copy-done.1, bf16[128,48]{1,0:T(8,128)(2,1)S(1)} %copy-done), custom_call_target="tpu_custom_call" | custom-call | tf_op jit(solution)/shard_map/arnoldi_step/pallas_call | solution.py:393
  49.2 0.6 %copy.10 = f32[4,128]{1,0:T(4,128)} copy(f32[4,128]{1,0:T(4,128)S(1)} %get-tuple-element.4) | data formatting | bytes 4096
  49.8 0.6 %copy.11 = f32[4,31]{1,0:T(4,128)} copy(f32[4,31]{1,0:T(4,128)S(1)} %get-tuple-element.5) | data formatting | bytes 992
Async XLA Ops:
  0.6 0.9 %copy-start = (bf16[128,48]{1,0:T(8,128)(2,1)S(1)}, bf16[128,48]{1,0:T(8,128)(2,1)}, u32[]{:S(2)}) copy-start(bf16[128,48]{1,0:T(8,128)(2,1)} %constant.5.clone.target_sel) | copy-start | bytes 36868
  0.6 0.9 %copy-start.1 = (bf16[128,48]{1,0:T(8,128)(2,1)S(1)}, bf16[128,48]{1,0:T(8,128)(2,1)}, u32[]{:S(2)}) copy-start(bf16[128,48]{1,0:T(8,128)(2,1)} %constant.4.clone.source_sel) | copy-start | bytes 36868
  0.7 0.9 %copy-start.2 = (f32[3,128]{1,0:T(4,128)S(1)}, f32[3,128]{1,0:T(4,128)}, u32[]{:S(2)}) copy-start(f32[3,128]{1,0:T(4,128)} %centroids.1) | copy-start | bytes 4612
  0.7 0.9 %copy-start.3 = (f32[128]{0:T(128)S(1)}, f32[128]{0:T(128)}, u32[]{:S(2)}) copy-start(f32[128]{0:T(128)} %param.6) | copy-start | bytes 1540
